TPU v7x, 512 devices: a whole 4x4x16 slice. The times are simulated.
512 devices in a mesh: ctx: 32 (over x, y, core), head: 16 (over z).
Axes of the slice: x: 4, y: 4, z: 16, core: 2. Of those that a mesh axis runs over, the one named last changes fastest.
Arguments:
- queries: bfloat16 [8192, 8192], P(('ctx', 'head')), may hold values from -160 to 160
- image_feats: bfloat16 [4096, 8192], P('ctx', 'head'), may hold values from -6 to 6
- key_value_weight: bfloat16 [8192, 2048], P('head'), may hold values from -0.0625 to 0.0625
- output_gradient: bfloat16 [8192, 8192], P(('ctx', 'head')), may hold values from -6 to 6
- spans: int32 [32, 2], replicated, may hold values from 0 to 8192, as said below
Outputs:
- query_grad: bfloat16 [8192, 8192], P(('ctx', 'head'))
- weight_grad: bfloat16 [8192, 2048], P(('head', 'ctx'))
Inputs may be any that keep to these rules, and one draw needn't show every extreme that they name: For image i, 256 * i <= spans[i, 0] < spans[i, 1] <= min(256 * (i + 2), 8192); in every draw some image spans that whole range.
All inputs are finite; a program needn't handle non-finite values.
Results may differ from a plain program's by a relative error of at most 0.029.
The roundings to bfloat16 on the way count: a program that leaves them out, or rounds other values in their place, can miss the bound.
Values may be sent and summed in bfloat16 or wider, within the bound.
A program may use at most 64 MiB of HBM per device.

v0:
```python
import math

import jax
import jax.numpy as jnp
from jax import lax
from jax.sharding import PartitionSpec as P

QUERY_HEADS = 64
KEY_VALUE_HEADS = 8
HEAD_SIZE = 128


NEG_FILL = -1e30


def passed_along(array, axis, by):
    size = lax.axis_size(axis)
    pairs = [(i, i + by) for i in range(size) if 0 <= i + by < size]
    return lax.ppermute(array, axis, pairs)


def attend_grads(query_rows, grad_rows, key_rows, value_rows, allowed, scaling):
    scores = (
        jnp.einsum("tkgd,skd->kgts", query_rows, key_rows, preferred_element_type=jnp.float32)
        * scaling
    )
    scores = jnp.where(allowed, scores, NEG_FILL)
    row_max = jnp.max(scores, axis=-1, keepdims=True)
    weights = jnp.exp(scores - row_max)
    attn_prob = weights / jnp.sum(weights, axis=-1, keepdims=True)
    has_key = jnp.any(allowed, axis=-1)
    attn_prob = jnp.where(has_key[:, None], attn_prob, 0.0)
    prob_low = attn_prob.astype(jnp.bfloat16)
    attended = jnp.einsum(
        "kgts,skd->tkgd", prob_low, value_rows, preferred_element_type=jnp.float32
    )
    row_dot = jnp.sum(grad_rows.astype(jnp.float32) * attended, axis=-1)
    grad_prob = jnp.einsum(
        "tkgd,skd->kgts", grad_rows, value_rows, preferred_element_type=jnp.float32
    )
    grad_score = attn_prob * (grad_prob - jnp.transpose(row_dot, (1, 2, 0))[..., None])
    score_low = grad_score.astype(jnp.bfloat16)
    grad_query = (
        jnp.einsum("kgts,skd->tkgd", score_low, key_rows, preferred_element_type=jnp.float32)
        * scaling
    )
    key_gradient = (
        jnp.einsum("kgts,tkgd->skd", score_low, query_rows, preferred_element_type=jnp.float32)
        * scaling
    )
    value_gradient = jnp.einsum(
        "kgts,tkgd->skd", prob_low, grad_rows, preferred_element_type=jnp.float32
    )
    return (grad_query.astype(jnp.bfloat16), key_gradient, value_gradient)


def per_device(queries, image_feats, key_value_weight, output_gradient, spans):
    heads_dev = lax.axis_size("head")
    ctx_count = lax.axis_size("ctx")
    head_idx = lax.axis_index("head")
    ctx_idx = lax.axis_index("ctx")
    q_dev = QUERY_HEADS // heads_dev
    query_group = QUERY_HEADS // KEY_VALUE_HEADS
    kv_dev = max(1, q_dev // query_group)
    q_per_kv = q_dev // kv_dev
    scaling = 1.0 / math.sqrt(HEAD_SIZE)
    image_token_rows = image_feats.shape[0]
    local_q, local_g = (
        lax.all_to_all(queries, "head", split_axis=1, concat_axis=0, tiled=True),
        lax.all_to_all(output_gradient, "head", split_axis=1, concat_axis=0, tiled=True),
    )
    text_rows = local_q.shape[0]
    query_rows = local_q.reshape(text_rows, kv_dev, q_per_kv, HEAD_SIZE)
    grad_rows = local_g.reshape(text_rows, kv_dev, q_per_kv, HEAD_SIZE)
    projected = jnp.dot(image_feats, key_value_weight, preferred_element_type=jnp.float32)
    first_kv = head_idx * q_dev // query_group
    full_kv = lax.psum(projected, "head")
    own_kv = lax.dynamic_slice_in_dim(
        full_kv, first_kv * 2 * HEAD_SIZE, kv_dev * 2 * HEAD_SIZE, 1
    ).astype(jnp.bfloat16)
    own_kv = own_kv.reshape(image_token_rows, kv_dev, 2, HEAD_SIZE)
    own_key = own_kv[:, :, 0, :]
    own_value = own_kv[:, :, 1, :]
    prev_key, prev_value = passed_along((own_key, own_value), "ctx", 1)
    key_rows = jnp.concatenate([prev_key, own_key], 0)
    value_rows = jnp.concatenate([prev_value, own_value], 0)
    text_pos = ctx_idx * text_rows + jnp.arange(text_rows, dtype=jnp.int32)
    prev_span = lax.dynamic_index_in_dim(spans, jnp.maximum(ctx_idx - 1, 0), 0, keepdims=False)
    own_span = lax.dynamic_index_in_dim(spans, ctx_idx, 0, keepdims=False)
    prev_ok = (ctx_idx > 0) & (text_pos >= prev_span[0]) & (text_pos < prev_span[1])
    own_ok = (text_pos >= own_span[0]) & (text_pos < own_span[1])
    allowed = jnp.concatenate(
        [
            jnp.broadcast_to(prev_ok[:, None], (text_rows, image_token_rows)),
            jnp.broadcast_to(own_ok[:, None], (text_rows, image_token_rows)),
        ],
        1,
    )
    head_queries = jnp.moveaxis(query_rows, 2, 0)[:, :, :, None, :]
    head_grads = jnp.moveaxis(grad_rows, 2, 0)[:, :, :, None, :]

    def one_head(inputs):
        query_one, grad_one = inputs
        return attend_grads(query_one, grad_one, key_rows, value_rows, allowed, scaling)

    stacked_q, stacked_k, stacked_v = lax.map(one_head, (head_queries, head_grads))
    grad_query = jnp.moveaxis(stacked_q[:, :, :, 0, :], 0, 2)
    key_gradient = jnp.sum(stacked_k, 0)
    value_gradient = jnp.sum(stacked_v, 0)
    query_grad = lax.all_to_all(
        grad_query.reshape(text_rows, q_dev * HEAD_SIZE),
        "head",
        split_axis=0,
        concat_axis=1,
        tiled=True,
    )
    grad_both = jnp.stack([key_gradient, value_gradient], 2).reshape(
        2 * image_token_rows, kv_dev * 2 * HEAD_SIZE
    )
    returned = passed_along(grad_both[:image_token_rows].astype(jnp.bfloat16), "ctx", -1).astype(
        jnp.float32
    )
    own_total = grad_both[image_token_rows:] + returned
    padded_rows = jnp.zeros((image_token_rows, 2 * KEY_VALUE_HEADS * HEAD_SIZE), jnp.float32)
    padded_rows = lax.dynamic_update_slice_in_dim(
        padded_rows, own_total, first_kv * 2 * HEAD_SIZE, 1
    )
    gradient_key_value = lax.psum(padded_rows.astype(jnp.bfloat16), "head")
    weight_sum = lax.psum_scatter(
        lax.dot_general(
            image_feats,
            gradient_key_value,
            (((0,), (0,)), ((), ())),
            preferred_element_type=jnp.float32,
        ).astype(jnp.bfloat16),
        "ctx",
        scatter_dimension=0,
        tiled=True,
    ).astype(jnp.float32)
    total_tokens = image_token_rows * ctx_count
    weight_grad = (weight_sum * (1.0 / math.sqrt(total_tokens))).astype(jnp.bfloat16)
    return (query_grad, weight_grad)


def solution(mesh):
    return jax.shard_map(
        per_device,
        mesh=mesh,
        in_specs=(
            P(("ctx", "head"), None),
            P("ctx", "head"),
            P("head", None),
            P(("ctx", "head"), None),
            P(),
        ),
        out_specs=(P(("ctx", "head"), None), P(("head", "ctx"), None)),
        check_vma=False,
    )
```

profile of v0, /device:TPU:1, one launch (start us, length us, event | category | flops | bytes accessed | tf_op | source)
XLA Modules:
  0.0 409.9 jit_solution(2957674637186548210)
XLA Ops:
  7.2 1.8 copy.59
  9.0 15.7 %all-to-all-start = ((bf16[16,16,512]{2,0,1:T(8,128)(2,1)}), bf16[16,16,512]{2,0,1:T(8,128)(2,1)S(1)}, u32[]{:S(2)}, u32[]{:S(2)}) async-start(bf16[16,16,512]{2,0,1:T(8,128)(2,1)} %bitcast.147), calls=%async_computation | async-start | bytes 524288 | tf_op jit(solution)/shard_map/all_to_all | solution.py:69
  24.8 1.3 fusion.43
  26.2 63.8 %all-reduce.4 = bf16[128,2048]{1,0:T(8,128)(2,1)} all-reduce(f32[128,2048]{1,0:T(8,128)S(1)} %fusion.43), channel_id=1, replica_groups=mesh['ctx'=32,'head'=16] {'head'}, use_global_device_ids=true, to_apply=%region_0.1 | all-reduce | flops 262144 | bytes 1572864 | tf_op jit(solution)/shard_map/psum | solution.py:77
  89.9 0.8 dynamic-slice_convert_fusion
  90.9 15.8 %collective-permute-start = (bf16[128,1,128]{2,0,1:T(8,128)(2,1)S(1)}, bf16[128,1,128]{2,0,1:T(8,128)(2,1)S(1)}, u32[]{:S(2)}, u32[]{:S(2)}) collective-permute-start(bf16[128,1,128]{2,0,1:T(8,128)(2,1)S(1)} %bitcast.203), channel_id=1, source_target_pairs={{0,16},{16,32},{32,48},{48,64},{64,80},{80,96},{96,112},{112,128},... | collective-permute-start | bytes 98312 | tf_op jit(solution)/shard_map/ppermute | solution.py:19
  106.8 1.9 collective-permute-start.1
  108.7 1.7 copy.58
  110.4 9.9 %all-to-all-start.1 = ((bf16[16,16,512]{2,0,1:T(8,128)(2,1)}), bf16[16,16,512]{2,0,1:T(8,128)(2,1)S(1)}, u32[]{:S(2)}, u32[]{:S(2)}) async-start(bf16[16,16,512]{2,0,1:T(8,128)(2,1)} %bitcast.146), calls=%async_computation.1 | async-start | bytes 524288 | tf_op jit(solution)/shard_map/all_to_all | solution.py:70
  120.4 0.6 fusion.41
  121.0 1.3 compare_and_fusion
  122.3 1.3 compare_and_fusion.1
  123.8 0.6 pad_maximum_fusion.2
  124.5 9.5 %all-to-all-done.1 = bf16[16,16,512]{2,0,1:T(8,128)(2,1)S(1)} async-done(((bf16[16,16,512]{2,0,1:T(8,128)(2,1)}), bf16[16,16,512]{2,0,1:T(8,128)(2,1)S(1)}, u32[]{:S(2)}, u32[]{:S(2)}) %all-to-all-start.1) | async-done | bytes 262176 | tf_op jit(solution)/shard_map/all_to_all | solution.py:70
  134.2 17.4 %while.15 = (s32[]{:T(128)}, bf16[4,256,1,1,128]{4,1,3,2,0:T(8,128)(2,1)}, f32[4,256,1,128]{1,3,2,0:T(8,128)S(1)}, f32[4,256,1,128]{1,3,2,0:T(8,128)}, pred[256]...) while((s32[]{:T(128)}, ...), condition=%wide.region_7.8_spmd, body=%wide.region_3.7_spmd.sunk | while | flops 102104320 | bytes 2701701 | solution.py:106
  134.2 0.2 fusion.77
  134.5 1.1 fusion.79
  135.6 1.0 fusion.80
  136.6 0.9 fusion.81
  137.7 0.9 fusion.83
  138.6 0.2 fusion.77
  138.9 1.1 fusion.79
  140.0 1.0 fusion.80
  141.0 0.9 fusion.81
  142.1 0.9 fusion.83
  142.9 0.2 fusion.77
  143.2 1.1 fusion.79
  144.3 1.0 fusion.80
  145.3 0.9 fusion.81
  146.4 0.9 fusion.83
  147.3 0.2 fusion.77
  147.6 1.1 fusion.79
  148.7 1.0 fusion.80
  149.7 0.9 fusion.81
  150.8 0.9 fusion.83
  151.6 1.1 reduce_sum.37
  152.8 7.4 %collective-permute-start.2 = (bf16[128,256]{0,1:T(8,128)(2,1)S(1)}, bf16[128,256]{0,1:T(8,128)(2,1)S(1)}, u32[]{:S(2)}, u32[]{:S(2)}) collective-permute-start(bf16[128,256]{0,1:T(8,128)(2,1)S(1)} %bitcast.207), channel_id=1, source_target_pairs={{16,0},{32,16},{48,32},{64,48},{80,64},{96,80},{112,96},{128,112},... | collective-permute-start | bytes 196616 | tf_op jit(solution)/shard_map/ppermute | solution.py:19
  160.2 3.1 collective-permute-done.2
  163.4 0.8 copy-done.1
  164.2 123.1 %all-reduce.3.cloned.1.call-done = bf16[128,2048]{0,1:T(8,128)(2,1)} async-done(((bf16[128,2048]{0,1:T(8,128)(2,1)}), bf16[128,2048]{0,1:T(8,128)(2,1)}) %all-reduce.3.cloned.1.call-update) | async-done | bytes 524304 | tf_op jit(solution)/shard_map/psum | solution.py:128
  287.4 3.1 fusion.36
  290.5 4.0 copy.47
  294.4 0.9 copy-done.3
  295.7 19.2 %all_to_all.51 = bf16[16,16,512]{2,1,0:T(8,128)(2,1)S(1)} all-to-all(bf16[16,16,512]{2,1,0:T(8,128)(2,1)S(1)} %all_to_all.44), channel_id=1, replica_groups=mesh['ctx'=32,'head'=16] {'head'}, dimensions={0} | all-to-all | bytes 524288 | tf_op jit(solution)/shard_map/all_to_all | solution.py:110
  314.9 0.7 copy.53
  315.6 85.4 %reduce-scatter.4.cloned.1.call-done = bf16[16,2048]{1,0:T(8,128)(2,1)} async-done(((bf16[512,2048]{1,0:T(8,128)(2,1)}), bf16[16,2048]{1,0:T(8,128)(2,1)}) %reduce-scatter.4.cloned.1.call-update) | async-done | bytes 65552
  401.0 1.1 copy.48
  402.3 0.8 copy.43
  (50 shorter events, 2.5 us)
Async XLA Ops:
  7.2 17.6 %copy-start = (bf16[512,2048]{1,0:T(8,128)(2,1)S(1)}, bf16[512,2048]{1,0:T(8,128)(2,1)}, u32[]{:S(2)}) copy-start(bf16[512,2048]{1,0:T(8,128)(2,1)} %param.9) | copy-start | bytes 6291460
  9.0 101.4 %all-to-all-start = ((bf16[16,16,512]{2,0,1:T(8,128)(2,1)}), bf16[16,16,512]{2,0,1:T(8,128)(2,1)S(1)}, u32[]{:S(2)}, u32[]{:S(2)}) async-start(bf16[16,16,512]{2,0,1:T(8,128)(2,1)} %bitcast.147), calls=%async_computation | async-start | bytes 524288 | tf_op jit(solution)/shard_map/all_to_all | solution.py:69
  26.1 94.2 %copy-start.4 = (s32[32,2]{0,1:T(2,128)S(1)}, s32[32,2]{0,1:T(2,128)}, u32[]{:S(2)}) copy-start(s32[32,2]{0,1:T(2,128)} %param.11) | copy-start | bytes 772
  90.9 32.8 %collective-permute-start = (bf16[128,1,128]{2,0,1:T(8,128)(2,1)S(1)}, bf16[128,1,128]{2,0,1:T(8,128)(2,1)S(1)}, u32[]{:S(2)}, u32[]{:S(2)}) collective-permute-start(bf16[128,1,128]{2,0,1:T(8,128)(2,1)S(1)} %bitcast.203), channel_id=1, source_target_pairs={{0,16},{16,32},{32,48},{48,64},{64,80},{80,96},{96,112},{112,128},... | collective-permute-start | bytes 98312 | tf_op jit(solution)/shard_map/ppermute | solution.py:19
  106.8 17.0 %collective-permute-start.1 = (bf16[128,1,128]{2,0,1:T(8,128)(2,1)S(1)}, bf16[128,1,128]{2,0,1:T(8,128)(2,1)S(1)}, u32[]{:S(2)}, u32[]{:S(2)}) collective-permute-start(bf16[128,1,128]{2,0,1:T(8,128)(2,1)S(1)} %bitcast.205), channel_id=1, source_target_pairs={{0,16},{16,32},{32,48},{48,64},{64,80},{80,96},{96,112},{112,128},... | collective-permute-start | bytes 98312 | tf_op jit(solution)/shard_map/ppermute | solution.py:19
  110.4 23.6 %all-to-all-start.1 = ((bf16[16,16,512]{2,0,1:T(8,128)(2,1)}), bf16[16,16,512]{2,0,1:T(8,128)(2,1)S(1)}, u32[]{:S(2)}, u32[]{:S(2)}) async-start(bf16[16,16,512]{2,0,1:T(8,128)(2,1)} %bitcast.146), calls=%async_computation.1 | async-start | bytes 524288 | tf_op jit(solution)/shard_map/all_to_all | solution.py:70
  120.3 167.1 %all-reduce.3.cloned.1.call-start = ((), (), s32[]{:S(2)}) async-start(), calls=%async_computation.4 | async-start | bytes 1048576 | tf_op jit(solution)/shard_map/psum | solution.py:128
  151.6 135.7 %copy-start.2 = (bf16[128,512]{1,0:T(8,128)(2,1)S(1)}, bf16[128,512]{1,0:T(8,128)(2,1)}, u32[]{:S(2)}) copy-start(bf16[128,512]{1,0:T(8,128)(2,1)} %param.8) | copy-start | bytes 393220
  152.8 10.5 %collective-permute-start.2 = (bf16[128,256]{0,1:T(8,128)(2,1)S(1)}, bf16[128,256]{0,1:T(8,128)(2,1)S(1)}, u32[]{:S(2)}, u32[]{:S(2)}) collective-permute-start(bf16[128,256]{0,1:T(8,128)(2,1)S(1)} %bitcast.207), channel_id=1, source_target_pairs={{16,0},{32,16},{48,32},{64,48},{80,64},{96,80},{112,96},{128,112},... | collective-permute-start | bytes 196616 | tf_op jit(solution)/shard_map/ppermute | solution.py:19
  163.4 0.8 copy-start.1
  164.2 236.8 %reduce-scatter.4.cloned.1.call-start = ((), (), s32[]{:S(2)}) async-start(), calls=%async_computation.5 | async-start | bytes 2162688
  294.4 0.9 copy-start.3
Sparse Core Ops, SparseCore 0:
  164.3 123.0 all-reduce.2
  294.6 106.4 reduce-scatter.3
where the time goes:
time: 412 us; the launch traced here: 410 us
  waiting for transfers between devices  221 us (54%)
  blocking collectives  82.9 us (20%)
  starting transfers between devices  50.8 us (12%)
  matrix products  21.5 us (5%)
  between operations  14.3 us (3%)
  local copies, waits for them, and re-layouts  14.2 us (3%)
  other arithmetic  4.9 us (1%)
    psum x1, waiting for transfers between devices, per_device(): gradient_key_value = lax.psum(padded_rows.astype(jnp.bfloat16), 'head')  123 us
    unnamed x3, waiting for transfers between devices  85.5 us
    psum x1, blocking collectives, per_device(): full_kv = lax.psum(projected, 'head')  63.8 us
    ppermute x3, starting transfers between devices, passed_along(): return lax.ppermute(array, axis, pairs)  25.1 us
    all_to_all x1, blocking collectives, per_device(): lax.all_to_all(grad_query.reshape(text_rows, q_dev * HEAD_SIZE), 'head',...  19.2 us
    all_to_all x1, starting transfers between devices, per_device(): lax.all_to_all(queries, 'head', split_axis=1, concat_axis=0, tiled=True)  15.7 us
    all_to_all x1, starting transfers between devices, per_device(): lax.all_to_all(output_gradient, 'head', split_axis=1, concat_axis=0, tile...  9.86 us
    all_to_all x1, waiting for transfers between devices, per_device(): lax.all_to_all(output_gradient, 'head', split_axis=1, concat_axis=0, tile...  9.47 us
  transfers between devices with their start and end apart: 7, of which 4 were waited for; matrix products, arithmetic and copies ran while one was open for 2% of the time, Pallas kernels for 0%

commit v1 on v0

v1 whole, which is shorter than its diff:
```python
import functools
import math

import jax
import jax.numpy as jnp
from jax import lax
from jax.experimental import pallas as pl
from jax.experimental.pallas import tpu as pltpu
from jax.sharding import PartitionSpec as P

RING = 16
CTX = 32
SIDE = 4
HEADS = 64
KV_HEADS = 8
GROUP = HEADS // KV_HEADS
HEAD_SIZE = 128
TOKENS = 128
ROWS = 16
TEXT_PER_INDEX = 256
HALF = TOKENS // 2
NEG_FILL = -1e30
BF16 = jnp.bfloat16
F32 = jnp.float32


def remote(src, dst, send_sem, recv_sem, device):
    return pltpu.make_async_remote_copy(
        src_ref=src,
        dst_ref=dst,
        send_sem=send_sem,
        recv_sem=recv_sem,
        device_id=device,
        device_id_type=pl.DeviceIdType.MESH,
    )


def matmul(a, b, dims):
    return lax.dot_general(a, b, (dims, ((), ())), preferred_element_type=F32)


def kernel(
    q_hbm, f_hbm, w_hbm, g_hbm, spans,
    qg_hbm, wg_hbm,
    q_ref, f_ref, w_ref, g_ref, qg_ref, wg_ref, ft_ref,
    s1, r1, kv, own, pg_src, pg_dst, s2, r2, kvg,
    c1_src, c1_dst, c1_own, c2_src, c2_dst, c3_src, c3_dst, c3_own,
    in_sem, out_sem, send_sem,
    r1_sem, ag1_sem, prev_sem, pg_sem, r2_sem, ag2_sem, c1_sem, c2_sem, c3_sem,
):
    z = lax.axis_index("head")
    ctx = lax.axis_index("ctx")
    core = lax.rem(ctx, 2)
    chip = ctx // 2
    y = lax.rem(chip, SIDE)
    x = chip // SIDE

    def ring(offset):
        return lax.rem(z + (offset + 2 * RING), RING)

    def at_xy(dx, dy):
        px, py = lax.rem(x + dx, SIDE), lax.rem(y + dy, SIDE)
        return ((px * SIDE + py) * 2 + core, z)

    sides = ((ctx, ring(1)), (ctx, ring(-1)))
    later = (lax.rem(ctx + 1, CTX), z)
    earlier = (lax.rem(ctx + CTX - 1, CTX), z)
    partner = (chip * 2 + (1 - core), z)
    along_x = [at_xy(d, 0) for d in range(1, SIDE)]
    along_y = [at_xy(0, d) for d in range(1, SIDE)]

    loads = [
        pltpu.make_async_copy(src, dst, in_sem.at[n])
        for n, (src, dst) in enumerate(
            ((f_hbm, f_ref), (w_hbm, w_ref), (q_hbm, q_ref), (g_hbm, g_ref))
        )
    ]
    for load in loads:
        load.start()
    barrier = pltpu.get_barrier_semaphore()
    met = (*sides, later, earlier, *along_x, *along_y)
    for device in met:
        pl.semaphore_signal(
            barrier, inc=1, device_id=device, device_id_type=pl.DeviceIdType.MESH
        )
    loads[0].wait()
    loads[1].wait()

    def projected(chunk):
        columns = pl.ds(pl.multiple_of(chunk * HEAD_SIZE, HEAD_SIZE), HEAD_SIZE)
        return matmul(f_ref[...], w_ref[:, columns], ((1,), (0,)))

    halves = (pl.ds(0, HALF), pl.ds(HALF, HALF))

    def send1(way, step, half):
        remote(
            s1.at[way, step, halves[half]], r1.at[way, step, halves[half]],
            send_sem.at[0], r1_sem.at[way, step, half], sides[way],
        ).start()

    def wait1(way, step, half):
        remote(
            s1.at[way, step, halves[half]], r1.at[way, step, halves[half]],
            send_sem.at[0], r1_sem.at[way, step, half], sides[way],
        ).wait_recv()

    first = projected(ring(8))
    s1[0, 0] = first
    s1[1, 0] = first
    pl.semaphore_wait(barrier, len(met))
    send1(0, 0, 0)
    send1(1, 0, 1)
    for step in range(1, 8):
        for way in range(2):
            s1[way, step] = projected(ring(8 - step if way == 0 else 8 + step))
        if step == 1:
            send1(0, 1, 1)
            send1(1, 1, 0)
        for half in range(2):
            for way in range(2):
                if step == 1 and half != way:
                    continue
                wait1(way, step - 1, half)
                s1[way, step, halves[half]] += r1[way, step - 1, halves[half]]
                send1(way, step, half)
    mine = projected(z)
    turned = f_ref[...].astype(F32).T.astype(BF16)
    for n in range(CTX):
        ft_ref[n % 2, pl.ds((n // 2) * ROWS, ROWS), :] = turned[n * ROWS : (n + 1) * ROWS]
    for half in range(2):
        for way in range(2):
            wait1(way, 7, half)
    kv[z, pl.ds(TOKENS, TOKENS)] = (mine + r1[0, 7] + r1[1, 7]).astype(BF16)

    own_rows = pl.ds(TOKENS, TOKENS)
    own_halves = (pl.ds(TOKENS, HALF), pl.ds(TOKENS + HALF, HALF))

    def gather1(way, step):
        owner = ring(-step if way == 0 else step)
        rows = own_rows if step < 7 else own_halves[way]
        block = kv.at[owner, rows]
        return remote(block, block, send_sem.at[1], ag1_sem.at[way, step], sides[way])

    def arrive1(way, step):
        owner = ring(-1 - step if way == 0 else 1 + step)
        rows = own_rows if step < 7 else own_halves[way]
        block = kv.at[owner, rows]
        remote(block, block, send_sem.at[1], ag1_sem.at[way, step], sides[way]).wait_recv()

    def pass_on(chunk):
        return remote(
            kv.at[chunk, own_rows], kv.at[chunk, pl.ds(0, TOKENS)],
            send_sem.at[2], prev_sem.at[chunk], later,
        )

    gather1(0, 0).start()
    gather1(1, 0).start()
    pass_on(z).start()
    loads[2].wait()
    loads[3].wait()

    lane = lax.broadcasted_iota(jnp.int32, (1, TOKENS), 1)
    text_pos = ctx * TEXT_PER_INDEX + z * ROWS + lax.rem(lane, ROWS)
    before = jnp.maximum(ctx - 1, 0)
    prev_ok = (text_pos >= spans[before, 0]) & (text_pos < spans[before, 1]) & (ctx > 0)
    own_ok = (text_pos >= spans[ctx, 0]) & (text_pos < spans[ctx, 1])
    scaling = 1.0 / math.sqrt(HEAD_SIZE)
    is_own = lax.broadcasted_iota(jnp.int32, (2 * TOKENS, TOKENS), 0) >= TOKENS
    allowed = (is_own & own_ok) | (jnp.logical_not(is_own) & prev_ok)

    def stacked(ref, head):
        start = pl.multiple_of(head * (GROUP * HEAD_SIZE), HEAD_SIZE)
        block = ref[:, pl.ds(start, GROUP * HEAD_SIZE)]
        return jnp.concatenate(
            [block[:, n * HEAD_SIZE : (n + 1) * HEAD_SIZE] for n in range(GROUP)], 0
        )

    def attend(head):
        for n in range(2):
            pass_on(2 * head + n).wait_recv()
        keys, values = kv[2 * head], kv[2 * head + 1]
        query, grad = stacked(q_ref, head), stacked(g_ref, head)
        scores = matmul(keys, query, ((1,), (1,))) * scaling
        scores = jnp.where(allowed, scores, NEG_FILL)
        grad_prob = matmul(values, grad, ((1,), (1,)))
        weights = jnp.exp(scores - jnp.max(scores, 0, keepdims=True))
        probs = weights / jnp.sum(weights, 0, keepdims=True)
        probs = jnp.where(allowed, probs, 0.0)
        prob_low = probs.astype(BF16)
        row_dot = jnp.sum(prob_low.astype(F32) * grad_prob, 0, keepdims=True)
        score_low = (probs * (grad_prob - row_dot)).astype(BF16)
        key_grad = matmul(score_low, query, ((1,), (0,))) * scaling
        value_grad = matmul(prob_low, grad, ((1,), (0,)))
        pg_src[2 * head] = key_grad[:TOKENS].astype(BF16)
        pg_src[2 * head + 1] = value_grad[:TOKENS].astype(BF16)
        send_back(head).start()
        own[2 * head] = key_grad[TOKENS:]
        own[2 * head + 1] = value_grad[TOKENS:]
        query_grad = (matmul(score_low, keys, ((0,), (0,))) * scaling).astype(BF16)
        start = pl.multiple_of(head * (GROUP * HEAD_SIZE), HEAD_SIZE)
        qg_ref[:, pl.ds(start, GROUP * HEAD_SIZE)] = jnp.concatenate(
            [query_grad[n * ROWS : (n + 1) * ROWS] for n in range(GROUP)], 1
        )

    def send_back(head):
        pair = pl.ds(2 * head, 2)
        return remote(
            pg_src.at[pair], pg_dst.at[pair], send_sem.at[3], pg_sem.at[head], earlier
        )

    turn = 2 * lax.rem(z, 2) - 1

    def head_at(k):
        offset = ((k + 1) // 2) * (1 if k % 2 else -1)
        return lax.rem(z // 2 + turn * offset + KV_HEADS, KV_HEADS)

    def copy2(way, step):
        rows = halves[way] if step == 0 else pl.ds(0, TOKENS)
        return remote(
            s2.at[way, step, rows], r2.at[way, step, rows],
            send_sem.at[4], r2_sem.at[way, step], sides[way],
        )

    def reduce2(step):
        send_back(head_at(step)).wait_recv()
        if step == 0:
            total = (own[z] + pg_dst[z].astype(F32)).astype(BF16)
            s2[0, 0] = total
            s2[1, 0] = total
            copy2(0, 0).start()
            copy2(1, 0).start()
            return
        for way in range(2):
            chunk = ring(-step if way == 0 else step)
            total = own[chunk] + pg_dst[chunk].astype(F32)
            copy2(way, step - 1).wait_recv()
            if step == 1:
                got = r2[way, 0, halves[way]].astype(F32)
                mixed = total[way * HALF : (way + 1) * HALF] + got
                s2[way, 1, halves[way]] = mixed.astype(BF16)
                rest = 1 - way
                s2[way, 1, halves[rest]] = total[rest * HALF : (rest + 1) * HALF].astype(BF16)
            else:
                s2[way, step] = (total + r2[way, step - 1].astype(F32)).astype(BF16)
            copy2(way, step).start()

    for step in range(8):
        arrive1(0, step)
        arrive1(1, step)
        if step < 7:
            gather1(0, step + 1).start()
            gather1(1, step + 1).start()
            pass_on(ring(-1 - step)).start()
            pass_on(ring(1 + step)).start()
        else:
            pass_on(ring(8)).start()
        attend(head_at(step))
        if step >= 1:
            reduce2(step - 1)
    out_q = pltpu.make_async_copy(qg_ref, qg_hbm, out_sem.at[0])
    out_q.start()
    reduce2(7)
    chunk = ring(8)
    total = own[chunk] + pg_dst[chunk].astype(F32)
    copy2(0, 7).wait_recv()
    copy2(1, 7).wait_recv()
    kvg[chunk] = (total + r2[0, 7].astype(F32) + r2[1, 7].astype(F32)).astype(BF16)

    def gather2(way, step):
        owner = ring(8 - step if way == 0 else 8 + step)
        rows = pl.ds(0, TOKENS) if step < 7 else halves[way]
        block = kvg.at[owner, rows]
        return remote(block, block, send_sem.at[5], ag2_sem.at[way, step], sides[way])

    def arrive2(way, step):
        owner = ring(7 - step if way == 0 else 9 + step)
        rows = pl.ds(0, TOKENS) if step < 7 else halves[way]
        block = kvg.at[owner, rows]
        remote(block, block, send_sem.at[5], ag2_sem.at[way, step], sides[way]).wait_recv()

    def copy_c1(k):
        return remote(c1_src.at[k], c1_dst.at[k], send_sem.at[6], c1_sem.at[k], partner)

    def copies_c2(k):
        found = []
        for d in range(1, SIDE):
            px, py = lax.rem(x + d, SIDE), lax.rem(y + d, SIDE)
            found.append(remote(
                c2_src.at[k, 0, px], c2_dst.at[k, 0, d - 1],
                send_sem.at[7], c2_sem.at[k, 0, d - 1], along_x[d - 1],
            ))
            found.append(remote(
                c2_src.at[k, 1, :, py], c2_dst.at[k, 1, d - 1],
                send_sem.at[7], c2_sem.at[k, 1, d - 1], along_y[d - 1],
            ))
        return found

    def copies_c3(k):
        found = []
        for d in range(1, SIDE):
            px, py = lax.rem(x + d, SIDE), lax.rem(y + d, SIDE)
            found.append(remote(
                c3_src.at[k, 0, py], c3_dst.at[k, 0, d - 1],
                send_sem.at[8], c3_sem.at[k, 0, d - 1], along_y[d - 1],
            ))
            found.append(remote(
                c3_src.at[k, 1, px], c3_dst.at[k, 1, d - 1],
                send_sem.at[8], c3_sem.at[k, 1, d - 1], along_x[d - 1],
            ))
        return found

    def chunks_of(k):
        return ring(8 + k), ring(7 - k)

    def stage1(k):
        a, b = chunks_of(k)
        both = jnp.concatenate([kvg[a], kvg[b]], 1)
        other = matmul(ft_ref[1 - core], both, ((1,), (0,))).astype(BF16)
        for n in range(2):
            part = other[:, n * HEAD_SIZE : (n + 1) * HEAD_SIZE]
            c1_src[k, n] = part.reshape(SIDE, SIDE, ROWS, HEAD_SIZE)
        copy_c1(k).start()
        kept = matmul(ft_ref[core], both, ((1,), (0,)))
        for n in range(2):
            part = kept[:, n * HEAD_SIZE : (n + 1) * HEAD_SIZE]
            c1_own[k, n] = part.reshape(SIDE, SIDE, ROWS, HEAD_SIZE)

    def stage2(k):
        copy_c1(k).wait_recv()
        total = c1_own[k] + c1_dst[k].astype(F32)
        c1_own[k] = total
        c2_src[k] = total.astype(BF16)
        for copy in copies_c2(k):
            copy.start()

    def stage3(k):
        for copy in copies_c2(k):
            copy.wait_recv()
        for n, mine in enumerate((c1_own[k, 0, x], c1_own[k, 1, :, y])):
            total = mine
            for d in range(SIDE - 1):
                total = total + c2_dst[k, n, d].astype(F32)
            c3_own[k, n] = total
            c3_src[k, n] = total.astype(BF16)
        for copy in copies_c3(k):
            copy.start()

    def stage4(k):
        for copy in copies_c3(k):
            copy.wait_recv()
        for n, (mine, chunk) in enumerate(zip((c3_own[k, 0, y], c3_own[k, 1, x]), chunks_of(k))):
            total = mine
            for d in range(SIDE - 1):
                total = total + c3_dst[k, n, d].astype(F32)
            total = total * (1.0 / math.sqrt(CTX * TOKENS))
            columns = pl.ds(pl.multiple_of(chunk * HEAD_SIZE, HEAD_SIZE), HEAD_SIZE)
            wg_ref[:, columns] = total.astype(BF16)

    for step in range(12):
        if 1 <= step <= 8:
            arrive2(0, step - 1)
            arrive2(1, step - 1)
        if step <= 7:
            gather2(0, step).start()
            gather2(1, step).start()
        if 0 <= step - 1 <= 7:
            stage1(step - 1)
        if 0 <= step - 2 <= 7:
            stage2(step - 2)
        if 0 <= step - 3 <= 7:
            stage3(step - 3)
        if 0 <= step - 4 <= 7:
            stage4(step - 4)
    out_w = pltpu.make_async_copy(wg_ref, wg_hbm, out_sem.at[1])
    out_w.start()

    chunks = pl.ds(0, RING - 1)
    sent = (
        s1.reshape(16, TOKENS, HEAD_SIZE).at[chunks],
        kv.at[chunks, pl.ds(0, TOKENS)],
        pg_src,
        pg_src,
        pg_src.at[chunks],
        pg_src.at[chunks],
        c1_src,
        c2_dst,
        c3_dst,
    )
    for n, block in enumerate(sent):
        remote(block, block, send_sem.at[n], in_sem.at[0], later).wait_send()
    out_q.wait()
    out_w.wait()


def per_device(queries, image_feats, key_value_weight, output_gradient, spans):
    anywhere = pl.BlockSpec(memory_space=pl.ANY)
    chunk = (TOKENS, HEAD_SIZE)
    tile = (ROWS, HEAD_SIZE)
    dma = pltpu.SemaphoreType.DMA
    vmem = pltpu.VMEM
    return pl.pallas_call(
        kernel,
        out_shape=(
            jax.ShapeDtypeStruct(queries.shape, BF16),
            jax.ShapeDtypeStruct((ROWS, 2048), BF16),
        ),
        in_specs=[anywhere] * 4 + [pl.BlockSpec(memory_space=pltpu.SMEM)],
        out_specs=(anywhere, anywhere),
        scratch_shapes=[
            vmem(queries.shape, BF16),
            vmem(image_feats.shape, BF16),
            vmem(key_value_weight.shape, BF16),
            vmem(output_gradient.shape, BF16),
            vmem(queries.shape, BF16),
            vmem((ROWS, 2048), BF16),
            vmem((2, 256, TOKENS), BF16),
            vmem((2, 8, *chunk), F32),
            vmem((2, 8, *chunk), F32),
            vmem((RING, 2 * TOKENS, HEAD_SIZE), BF16),
            vmem((RING, *chunk), F32),
            vmem((RING, *chunk), BF16),
            vmem((RING, *chunk), BF16),
            vmem((2, 8, *chunk), BF16),
            vmem((2, 8, *chunk), BF16),
            vmem((RING, *chunk), BF16),
            vmem((8, 2, SIDE, SIDE, *tile), BF16),
            vmem((8, 2, SIDE, SIDE, *tile), BF16),
            vmem((8, 2, SIDE, SIDE, *tile), F32),
            vmem((8, 2, SIDE, SIDE, *tile), BF16),
            vmem((8, 2, SIDE - 1, SIDE, *tile), BF16),
            vmem((8, 2, SIDE, *tile), BF16),
            vmem((8, 2, SIDE - 1, *tile), BF16),
            vmem((8, 2, SIDE, *tile), F32),
            dma((4,)),
            dma((2,)),
            dma((9,)),
            dma((2, 8, 2)),
            dma((2, 8)),
            dma((RING,)),
            dma((KV_HEADS,)),
            dma((2, 8)),
            dma((2, 8)),
            dma((8,)),
            dma((8, 2, 3)),
            dma((8, 2, 3)),
        ],
        compiler_params=pltpu.CompilerParams(
            collective_id=0, has_side_effects=True, vmem_limit_bytes=40 * 1024 * 1024
        ),
    )(queries, image_feats, key_value_weight, output_gradient, spans)


def solution(mesh):
    return jax.shard_map(
        per_device,
        mesh=mesh,
        in_specs=(
            P(("ctx", "head"), None),
            P("ctx", "head"),
            P("head", None),
            P(("ctx", "head"), None),
            P(),
        ),
        out_specs=(P(("ctx", "head"), None), P(("head", "ctx"), None)),
        check_vma=False,
    )
```

time: 412 us -> 131 us (0.32)
  waiting for transfers between devices: 221 us -> 0 us
  Pallas kernels: 0 us -> 123 us
  blocking collectives: 82.9 us -> 0 us
  starting transfers between devices: 50.8 us -> 0 us
  matrix products: 21.5 us -> 0 us
  between operations: 14.3 us -> 0.64 us
  local copies, waits for them, and re-layouts: 14.2 us -> 6.49 us
  other arithmetic: 4.9 us -> 0 us
    pallas_call x0 -> x1, Pallas kernels: none -> 123 us  [per_device(): pl.pallas_call(kernel, out_shape=(jax.ShapeDtypeStruct(queries.shape, BF1...]
    psum x1 -> x0, waiting for transfers between devices: 123 us -> none  [per_device(): gradient_key_value = lax.psum(padded_rows.astype(jnp.bfloat16), 'head')]
    unnamed x3 -> x0, waiting for transfers between devices: 85.5 us -> none
    psum x1 -> x0, blocking collectives: 63.8 us -> none  [per_device(): full_kv = lax.psum(projected, 'head')]
    all_to_all x2 -> x0, starting transfers between devices: 25.6 us -> none  [the longest x1 15.7 us: per_device(): lax.all_to_all(queries, 'head', split_axis=1, concat_axis=0, tiled=True)]
    ppermute x3 -> x0, starting transfers between devices: 25.1 us -> none  [passed_along(): return lax.ppermute(array, axis, pairs)]
    dot_general x26 -> x0, matrix products: 21.5 us -> none  [the longest x4 4.31 us: attend_grads(): jnp.einsum('kgts,skd->tkgd', prob_low, value_rows, preferred_element_type...]
    all_to_all x1 -> x0, blocking collectives: 19.2 us -> none  [per_device(): lax.all_to_all(grad_query.reshape(text_rows, q_dev * HEAD_SIZE), 'head',...]
  transfers between devices with their start and end apart: 7 -> 0, of which waited for: 4 -> 0; matrix products, arithmetic and copies ran while one was open for 2% -> 0% of each run, Pallas kernels for 0% -> 0%
where the time goes in v1:
time: 131 us; the launch traced here: 130 us
  Pallas kernels  123 us (94%)
  local copies, waits for them, and re-layouts  6.49 us (5%)
    pallas_call x1, Pallas kernels, per_device(): pl.pallas_call(kernel, out_shape=(jax.ShapeDtypeStruct(queries.shape, BF1...  123 us
    unnamed x11, local copies, waits for them, and re-layouts  6.49 us

profile of v1, /device:TPU:1, one launch (start us, length us, event | category | flops | bytes accessed | tf_op | source)
XLA Modules:
  0.0 130.4 jit_solution(5387256139758179387)
XLA Ops:
  0.6 0.8 copy.7.spans
  1.4 0.0 copy-start
  1.4 1.6 %copy-done = bf16[512,2048]{1,0:T(8,128)(2,1)S(1)} copy-done((bf16[512,2048]{1,0:T(8,128)(2,1)S(1)}, bf16[512,2048]{1,0:T(8,128)(2,1)}, u32[]{:S(2)}) %copy-start) | copy-done | bytes 2097176
  3.0 0.0 copy-start.1
  3.0 0.9 copy-done.1
  3.9 0.0 copy-start.2
  3.9 0.9 copy-done.2
  4.9 0.0 copy-start.3
  4.9 0.9 copy-done.3
  5.8 123.2 %shard_map.68 = (bf16[16,8192]{1,0:T(8,128)(2,1)S(1)}, bf16[16,2048]{1,0:T(8,128)(2,1)S(1)}) custom-call(bf16[16,8192]{1,0:T(8,128)(2,1)S(1)} %copy-done.1, bf16[128,512]{1,0:T(8,128)(2,1)S(1)} %copy-done.3, bf16[512,2048]{1,0:T(8,128)(2,1)S(1)} %copy-done, bf16[16,8192]{1,0:T(8,128)(2,1)S(1)} %copy-done.2, s32[32,2]{1,0:T(8,128)S(1)} %copy.7.spans), custom_call_target="tpu_custom_call" | custom-call | tf_op jit(solution)/shard_map/pallas_call | solution.py:401
  129.0 0.7 copy.10
  129.7 0.6 copy.11
Async XLA Ops:
  1.4 1.6 %copy-start = (bf16[512,2048]{1,0:T(8,128)(2,1)S(1)}, bf16[512,2048]{1,0:T(8,128)(2,1)}, u32[]{:S(2)}) copy-start(bf16[512,2048]{1,0:T(8,128)(2,1)} %w_hbm.1) | copy-start | bytes 6291460
  3.0 0.9 copy-start.1
  3.9 0.9 copy-start.2
  4.9 0.9 copy-start.3

commit v2 on v1

v2 whole, which is shorter than its diff:
```python
import math

import jax
import jax.numpy as jnp
from jax import lax
from jax.experimental import pallas as pl
from jax.experimental.pallas import tpu as pltpu
from jax.sharding import PartitionSpec as P

RING = 16
CTX = 32
SIDE = 4
CHIPS = SIDE * SIDE
HEAD_SIZE = 128
KV_HEADS = 8
GROUP = 8
WIDE = GROUP * HEAD_SIZE
TOKENS = 128
ROWS = 16
TEXT_PER_INDEX = 256
HALF = TOKENS // 2
NEG_FILL = -1e30
BF16 = jnp.bfloat16
F32 = jnp.float32

SPREAD = {3: 0, 1: 0, 6: 3, 4: 3, 2: 3, 8: 6, 7: 6, 5: 6}
GATHER = {3: 0, 1: 0, 6: 3, 4: 3, 2: 3, 8: 6, 7: 6, 5: 6}
GATHER_INNER = (6, 3)


def children(tree, place):
    return [q for q, p in tree.items() if p == place]


def remote(src, dst, send_sem, recv_sem, device):
    return pltpu.make_async_remote_copy(
        src_ref=src,
        dst_ref=dst,
        send_sem=send_sem,
        recv_sem=recv_sem,
        device_id=device,
        device_id_type=pl.DeviceIdType.MESH,
    )


def matmul(a, b, dims):
    return lax.dot_general(a, b, (dims, ((), ())), preferred_element_type=F32)


def kernel(
    q_hbm, f_hbm, w_hbm, g_hbm, spans_hbm,
    qg_hbm, wg_hbm,
    spans, f_ref, w_ref, q_ref, g_ref, qg_ref, wg_ref, ft_src, ft_ref,
    part, r1, kv, own, pg_src, pg_dst, s2, r2, kvg,
    c2_own, c2_src, c2_dst,
    in_sem, out_sem, send_sem,
    ft_sem, r1_sem, ag1_sem, prev_sem, pg_sem, r2_sem, ag2_sem, c1_sem, c2_sem,
):
    z = lax.axis_index("head")
    ctx = lax.axis_index("ctx")
    core = lax.rem(ctx, 2)
    chip = ctx // 2
    y = lax.rem(chip, SIDE)
    x = chip // SIDE

    def ring(offset):
        return lax.rem(z + (offset + 2 * RING), RING)

    def chip_at(n):
        return lax.rem(x + n // SIDE, SIDE) * SIDE + lax.rem(y + n % SIDE, SIDE)

    later = (lax.rem(ctx + 1, CTX), z)
    earlier = (lax.rem(ctx + CTX - 1, CTX), z)
    partner = (chip * 2 + (1 - core), z)

    loads = [
        pltpu.make_async_copy(src, dst, in_sem.at[n])
        for n, (src, dst) in enumerate(
            ((f_hbm, f_ref), (w_hbm, w_ref), (q_hbm, q_ref), (g_hbm, g_ref), (spans_hbm, spans))
        )
    ]
    for load in loads:
        load.start()
    barrier = pltpu.get_barrier_semaphore()
    met = [(ctx, ring(d)) for d in (1, 2, 3, -1, -2, -3)] + [later, earlier]
    met += [(chip_at(n) * 2 + core, z) for n in range(1, CHIPS)]
    for device in met:
        pl.semaphore_signal(
            barrier, inc=1, device_id=device, device_id_type=pl.DeviceIdType.MESH
        )
    loads[0].wait()
    loads[1].wait()
    both_sides = (0, 1)
    halves = (pl.ds(0, HALF), pl.ds(HALF, HALF))
    whole = pl.ds(0, TOKENS)

    def rows_at(side, place):
        return halves[side] if place == 8 else whole

    def project(chunk):
        columns = pl.ds(pl.multiple_of(chunk * HEAD_SIZE, HEAD_SIZE), HEAD_SIZE)
        part[chunk] = matmul(f_ref[...], w_ref[:, columns], ((1,), (0,)))

    def up1(side, place, half):
        way = 1 - 2 * side
        owner = ring(-way * place)
        target = ring(-way * (place - GATHER[place]))
        return remote(
            part.at[owner, halves[half]], r1.at[side, place - 1, halves[half]],
            send_sem.at[0], r1_sem.at[side, place - 1, half], (ctx, target),
        )

    def send1(half, *places):
        for place in places:
            for side in both_sides:
                if place < 8 or side == half:
                    up1(side, place, half).start()

    def sum1(half, place):
        for side in both_sides:
            way = 1 - 2 * side
            owner = ring(-way * place)
            for q in children(GATHER, place):
                if q < 8 or side == half:
                    up1(side, q, half).wait_recv()
                    part[owner, halves[half]] += r1[side, q - 1, halves[half]]
            up1(side, place, half).start()

    project(ring(8))
    pl.semaphore_wait(barrier, len(met))
    send1(0, 8)
    for place in (7, 5):
        for side in both_sides:
            project(ring(place if side else -place))
        send1(0, place)
    send1(1, 8, 7, 5)
    for place in (6, 4, 2, 3, 1, 0):
        for side in both_sides:
            if place > 0 or side == 0:
                project(ring(place if side else -place))
    turned = f_ref[...].astype(F32).T.astype(BF16)
    image_lanes = pl.ds(pl.multiple_of(core * TOKENS, TOKENS), TOKENS)
    for n in range(CTX):
        ft_src[n % 2, pl.ds((n // 2) * ROWS, ROWS), :] = turned[n * ROWS : (n + 1) * ROWS]
    ft_ref[:, image_lanes] = ft_src[core]
    features = remote(
        ft_src.at[1 - core], ft_ref.at[:, image_lanes], send_sem.at[1], ft_sem.at[0], partner
    )
    features.start()
    sum1(0, 6)
    sum1(1, 6)
    send1(0, 4, 2)
    send1(1, 4, 2)
    sum1(0, 3)
    sum1(1, 3)
    send1(0, 1)
    send1(1, 1)

    own_rows, prev_rows = pl.ds(TOKENS, TOKENS), pl.ds(0, TOKENS)
    for half in range(2):
        total = part[z, halves[half]]
        for q in children(GATHER, 0):
            for side in both_sides:
                up1(side, q, half).wait_recv()
                total = total + r1[side, q - 1, halves[half]]
        kv[z, pl.ds(TOKENS + half * HALF, HALF)] = total.astype(BF16)

    def spread1(side, place, child, half):
        way = 1 - 2 * side
        block = kv.at[ring(-way * place), pl.ds(TOKENS + half * HALF, HALF)]
        target = ring(way * (child - place))
        return remote(
            block, block, send_sem.at[2], ag1_sem.at[side, child - 1, half], (ctx, target)
        )

    def forward1(side, place, half):
        for child in children(SPREAD, place):
            if child < 8 or side == half:
                spread1(side, place, child, half).start()

    def pass_on(chunk):
        return remote(
            kv.at[chunk, own_rows], kv.at[chunk, prev_rows],
            send_sem.at[3], prev_sem.at[chunk], later,
        )

    def take1(*places):
        for place in places:
            for half in range(2):
                for side in both_sides:
                    if place < 8 or side == half:
                        spread1(side, place, place, half).wait_recv()
                        forward1(side, place, half)
            for side in both_sides[: 1 if place == 8 else 2]:
                pass_on(ring(place if side else -place)).start()

    for half in range(2):
        for side in both_sides:
            forward1(side, 0, half)
    pass_on(z).start()
    loads[2].wait()
    loads[3].wait()
    loads[4].wait()

    lane = lax.broadcasted_iota(jnp.int32, (1, TOKENS), 1)
    token = ctx * TEXT_PER_INDEX + z * ROWS + lax.rem(lane, ROWS)
    before = jnp.maximum(ctx - 1, 0)
    prev_ok = (token >= spans[0, before]) & (token < spans[1, before]) & (ctx > 0)
    own_ok = (token >= spans[0, ctx]) & (token < spans[1, ctx])
    is_own = lax.broadcasted_iota(jnp.int32, (2 * TOKENS, TOKENS), 0) >= TOKENS
    allowed = (is_own & own_ok) | (jnp.logical_not(is_own) & prev_ok)
    scaling = 1.0 / math.sqrt(HEAD_SIZE)

    def stacked(ref, head):
        block = ref[:, pl.ds(pl.multiple_of(head * WIDE, WIDE), WIDE)]
        return jnp.concatenate(
            [block[:, n * HEAD_SIZE : (n + 1) * HEAD_SIZE] for n in range(GROUP)], 0
        )

    def attend(head):
        for n in range(2):
            pass_on(2 * head + n).wait_recv()
        keys, values = kv[2 * head], kv[2 * head + 1]
        query, grad = stacked(q_ref, head), stacked(g_ref, head)
        scores = matmul(keys, query, ((1,), (1,))) * scaling
        scores = jnp.where(allowed, scores, NEG_FILL)
        grad_prob = matmul(values, grad, ((1,), (1,)))
        weights = jnp.exp(scores - jnp.max(scores, 0, keepdims=True))
        probs = weights * (1.0 / jnp.sum(weights, 0, keepdims=True))
        probs = jnp.where(allowed, probs, 0.0)
        prob_low = probs.astype(BF16)
        row_dot = jnp.sum(prob_low.astype(F32) * grad_prob, 0, keepdims=True)
        score_low = (probs * (grad_prob - row_dot)).astype(BF16)
        key_grad = matmul(score_low, query, ((1,), (0,))) * scaling
        value_grad = matmul(prob_low, grad, ((1,), (0,)))
        pg_src[2 * head] = key_grad[:TOKENS].astype(BF16)
        pg_src[2 * head + 1] = value_grad[:TOKENS].astype(BF16)
        send_back(head).start()
        own[2 * head] = key_grad[TOKENS:]
        own[2 * head + 1] = value_grad[TOKENS:]
        query_grad = (matmul(score_low, keys, ((0,), (0,))) * scaling).astype(BF16)
        qg_ref[:, pl.ds(pl.multiple_of(head * WIDE, WIDE), WIDE)] = jnp.concatenate(
            [query_grad[n * ROWS : (n + 1) * ROWS] for n in range(GROUP)], 1
        )

    def send_back(head):
        pair = pl.ds(2 * head, 2)
        return remote(
            pg_src.at[pair], pg_dst.at[pair], send_sem.at[4], pg_sem.at[head], earlier
        )

    turn = 2 * lax.rem(z, 2) - 1

    def head_at(k):
        offset = ((k + 1) // 2) * (1 if k % 2 else -1)
        return lax.rem(z // 2 + turn * offset + KV_HEADS, KV_HEADS)

    def up2(side, place):
        way = 1 - 2 * side
        rows = rows_at(side, place)
        target = ring(-way * (place - GATHER[place]))
        return remote(
            s2.at[side, place - 1, rows], r2.at[side, place - 1, rows],
            send_sem.at[5], r2_sem.at[side, place - 1], (ctx, target),
        )

    def gathered(chunk):
        return own[chunk] + pg_dst[chunk].astype(F32)

    def leaf2(k):
        send_back(head_at(k)).wait_recv()
        place = 8 - k
        if place in GATHER_INNER:
            return
        for side in both_sides:
            way = 1 - 2 * side
            s2[side, place - 1] = gathered(ring(8 - way * place)).astype(BF16)
            up2(side, place).start()

    def inner2(place):
        for side in both_sides:
            way = 1 - 2 * side
            total = gathered(ring(8 - way * place))
            for q in children(GATHER, place):
                up2(side, q).wait_recv()
                if q == 8:
                    got = r2[side, 7, halves[side]].astype(F32)
                    mixed = total[side * HALF : (side + 1) * HALF] + got
                    rest = total[(1 - side) * HALF : (2 - side) * HALF]
                    total = jnp.concatenate([rest, mixed] if side else [mixed, rest], 0)
                else:
                    total = total + r2[side, q - 1].astype(F32)
            s2[side, place - 1] = total.astype(BF16)
            up2(side, place).start()

    take1(3, 1)
    attend(head_at(0))
    take1(6, 4, 2)
    leaf2(0)
    for k in (1, 2, 3):
        attend(head_at(k))
    take1(7, 5, 8)
    for k in (1, 2, 3):
        leaf2(k)
    for k in (4, 5, 6):
        attend(head_at(k))
    inner2(6)
    attend(head_at(7))
    out_q = pltpu.make_async_copy(qg_ref, qg_hbm, out_sem.at[0])
    out_q.start()
    for k in (4, 5, 6, 7):
        leaf2(k)
    inner2(3)
    total = gathered(ring(8))
    for q in children(GATHER, 0):
        for side in both_sides:
            up2(side, q).wait_recv()
            total = total + r2[side, q - 1].astype(F32)
    image_rows = pl.ds(pl.multiple_of(core * TOKENS, TOKENS), TOKENS)
    kvg[z, image_rows] = total.astype(BF16)

    def spread2(side, place, child, half):
        way = 1 - 2 * side
        start = pl.multiple_of(core * TOKENS + half * HALF, HALF)
        block = kvg.at[ring(-way * place), pl.ds(start, HALF)]
        target = ring(way * (child - place))
        return remote(
            block, block, send_sem.at[6], ag2_sem.at[side, child - 1, half], (ctx, target)
        )

    def forward2(side, place, half):
        for child in children(SPREAD, place):
            if child < 8 or side == half:
                spread2(side, place, child, half).start()

    def share(owner):
        block = kvg.at[owner, image_rows]
        return remote(block, block, send_sem.at[7], c1_sem.at[owner], partner)

    def shared(owner):
        block = kvg.at[owner, pl.ds(pl.multiple_of((1 - core) * TOKENS, TOKENS), TOKENS)]
        remote(block, block, send_sem.at[7], c1_sem.at[owner], partner).wait_recv()

    def take2(*places):
        for place in places:
            for half in range(2):
                for side in both_sides:
                    if place < 8 or side == half:
                        spread2(side, place, place, half).wait_recv()
                        forward2(side, place, half)
            for side in both_sides[: 1 if place == 8 else 2]:
                share(ring(place if side else -place)).start()

    def owners_of(place):
        return (z, ring(8)) if place == 8 else (ring(-place), ring(place))

    def copies_c2(k):
        return [
            remote(
                c2_src.at[k, chip_at(n)], c2_dst.at[k, n - 1],
                send_sem.at[8], c2_sem.at[k, n - 1], (chip_at(n) * 2 + core, z),
            )
            for n in range(1, CHIPS)
        ]

    def multiply(*places):
        for place in places:
            k = place - 1
            owners = owners_of(place)
            for owner in owners:
                shared(owner)
            product = matmul(
                ft_ref[...], jnp.concatenate([kvg[n] for n in owners], 1), ((1,), (0,))
            )
            c2_own[k] = product
            c2_src[k] = product.astype(BF16).reshape(CHIPS, ROWS, 2 * HEAD_SIZE)
            for copy in copies_c2(k):
                copy.start()

    def finish(place):
        k = place - 1
        total = c2_own[k, pl.ds(pl.multiple_of(chip * ROWS, ROWS), ROWS)]
        for n, copy in enumerate(copies_c2(k)):
            copy.wait_recv()
            total = total + c2_dst[k, n].astype(F32)
        total = (total * (1.0 / math.sqrt(CTX * TOKENS))).astype(BF16)
        for n, owner in enumerate(owners_of(place)):
            chunk = lax.rem(owner + 8, RING)
            columns = pl.ds(pl.multiple_of(chunk * HEAD_SIZE, HEAD_SIZE), HEAD_SIZE)
            wg_ref[:, columns] = total[:, n * HEAD_SIZE : (n + 1) * HEAD_SIZE]

    for half in range(2):
        for side in both_sides:
            forward2(side, 0, half)
    share(z).start()
    features.wait_recv()
    take2(3, 1)
    multiply(1, 3)
    take2(6, 4, 2)
    multiply(2, 4, 6)
    take2(7, 5)
    multiply(5, 7)
    take2(8)
    multiply(8)
    for place in (1, 3, 2, 4, 6, 5, 7, 8):
        finish(place)
    out_w = pltpu.make_async_copy(wg_ref, wg_hbm, out_sem.at[1])
    out_w.start()

    fifteen = pl.ds(0, RING - 1)
    sent = (
        part.at[fifteen],
        ft_src.at[0],
        pg_src.at[fifteen],
        pg_src,
        pg_src,
        pg_src.at[fifteen],
        pg_src.at[fifteen],
        pg_src,
        c2_dst,
    )
    for n, block in enumerate(sent):
        remote(block, block, send_sem.at[n], in_sem.at[0], partner).wait_send()
    out_q.wait()
    out_w.wait()


def settle(a_in, b_in, a_out, b_out):
    a_out[...] = a_in[...]
    b_out[...] = b_in[...]


def per_device(queries, image_feats, key_value_weight, output_gradient, spans):
    anywhere = pl.BlockSpec(memory_space=pl.ANY)
    chunk = (TOKENS, HEAD_SIZE)
    double = (2 * TOKENS, HEAD_SIZE)
    dma = pltpu.SemaphoreType.DMA
    vmem = pltpu.VMEM
    results = pl.pallas_call(
        kernel,
        out_shape=(
            jax.ShapeDtypeStruct(queries.shape, BF16),
            jax.ShapeDtypeStruct((ROWS, 2048), BF16),
        ),
        in_specs=[anywhere] * 5,
        out_specs=(anywhere, anywhere),
        scratch_shapes=[
            pltpu.SMEM((2, CTX), jnp.int32),
            vmem(image_feats.shape, BF16),
            vmem(key_value_weight.shape, BF16),
            vmem(queries.shape, BF16),
            vmem(output_gradient.shape, BF16),
            vmem(queries.shape, BF16),
            vmem((ROWS, 2048), BF16),
            vmem((2, 256, TOKENS), BF16),
            vmem((256, 2 * TOKENS), BF16),
            vmem((RING, *chunk), F32),
            vmem((2, 8, *chunk), F32),
            vmem((RING, *double), BF16),
            vmem((RING, *chunk), F32),
            vmem((RING, *chunk), BF16),
            vmem((RING, *chunk), BF16),
            vmem((2, 8, *chunk), BF16),
            vmem((2, 8, *chunk), BF16),
            vmem((RING, *double), BF16),
            vmem((8, 256, 2 * HEAD_SIZE), F32),
            vmem((8, CHIPS, ROWS, 2 * HEAD_SIZE), BF16),
            vmem((8, CHIPS - 1, ROWS, 2 * HEAD_SIZE), BF16),
            dma((5,)),
            dma((2,)),
            dma((9,)),
            dma((1,)),
            dma((2, 8, 2)),
            dma((2, 8, 2)),
            dma((RING,)),
            dma((KV_HEADS,)),
            dma((2, 8)),
            dma((2, 8, 2)),
            dma((RING,)),
            dma((8, CHIPS - 1)),
        ],
        compiler_params=pltpu.CompilerParams(
            collective_id=0, has_side_effects=True, vmem_limit_bytes=60 * 1024 * 1024
        ),
    )(queries, image_feats, key_value_weight, output_gradient, spans.T)
    inside = pl.BlockSpec(memory_space=pltpu.VMEM)
    return pl.pallas_call(
        settle,
        out_shape=tuple(jax.ShapeDtypeStruct(r.shape, r.dtype) for r in results),
        in_specs=[inside] * 2,
        out_specs=(inside, inside),
    )(*results)


def solution(mesh):
    return jax.shard_map(
        per_device,
        mesh=mesh,
        in_specs=(
            P(("ctx", "head"), None),
            P("ctx", "head"),
            P("head", None),
            P(("ctx", "head"), None),
            P(),
        ),
        out_specs=(P(("ctx", "head"), None), P(("head", "ctx"), None)),
        check_vma=False,
    )
```

time: 131 us -> 94.6 us (0.72)
  Pallas kernels: 123 us -> 93.8 us
  local copies, waits for them, and re-layouts: 6.49 us -> 0 us
    pallas_call x1, Pallas kernels: 123 us -> 92.1 us  [per_device(): pl.pallas_call(kernel, out_shape=(jax.ShapeDtypeStruct(queries.shape, BF1...]
    unnamed x11 -> x0, local copies, waits for them, and re-layouts: 6.49 us -> none
    pallas_call x0 -> x1, Pallas kernels: none -> 1.69 us  [per_device(): pl.pallas_call(settle, out_shape=tuple((jax.ShapeDtypeStruct(r.shape, r.d...]
where the time goes in v2:
time: 94.6 us; the launch traced here: 94.4 us
  Pallas kernels  93.8 us (99%)
    pallas_call x1, Pallas kernels, per_device(): pl.pallas_call(kernel, out_shape=(jax.ShapeDtypeStruct(queries.shape, BF1...  92.1 us

profile of v2, /device:TPU:1, one launch (start us, length us, event | category | flops | bytes accessed | tf_op | source)
XLA Modules:
  0.0 94.4 jit_solution(14849595528908197965)
XLA Ops:
  0.6 92.1 %shard_map.68 = (bf16[16,8192]{1,0:T(8,128)(2,1)}, bf16[16,2048]{1,0:T(8,128)(2,1)}) custom-call(bf16[16,8192]{1,0:T(8,128)(2,1)} %q_hbm.1, bf16[128,512]{1,0:T(8,128)(2,1)} %f_hbm.1, bf16[512,2048]{1,0:T(8,128)(2,1)} %w_hbm.1, bf16[16,8192]{1,0:T(8,128)(2,1)} %g_hbm.1, s32[2,32]{1,0:T(2,128)} %bitcast.1), custom_call_target="tpu_custom_call" | custom-call | tf_op jit(solution)/shard_map/pallas_call | solution.py:439
  92.7 1.7 %shard_map.69 = (bf16[16,8192]{1,0:T(8,128)(2,1)}, bf16[16,2048]{1,0:T(8,128)(2,1)}) custom-call(bf16[16,8192]{1,0:T(8,128)(2,1)} %get-tuple-element.4.a_in, bf16[16,2048]{1,0:T(8,128)(2,1)} %get-tuple-element.5.b_in), custom_call_target="tpu_custom_call" | custom-call | tf_op jit(solution)/shard_map/pallas_call | solution.py:487

commit v3 on v2

--- a/solution.py
+++ b/solution.py
@@ -23,8 +23,9 @@
 BF16 = jnp.bfloat16
 F32 = jnp.float32
 
-SPREAD = {3: 0, 1: 0, 6: 3, 4: 3, 2: 3, 8: 6, 7: 6, 5: 6}
-GATHER = {3: 0, 1: 0, 6: 3, 4: 3, 2: 3, 8: 6, 7: 6, 5: 6}
+SPREAD = {3: 0, 2: 0, 1: 0, 6: 3, 5: 3, 4: 3, 8: 6, 7: 6}
+GATHER = {3: 0, 2: 0, 1: 0, 6: 3, 5: 3, 4: 3, 8: 6, 7: 6}
+PROJECT = {3: 0, 1: 0, 6: 3, 4: 3, 2: 3, 8: 6, 7: 6, 5: 6}
 GATHER_INNER = (6, 3)
 
 
@@ -92,10 +93,6 @@
     loads[1].wait()
     both_sides = (0, 1)
     halves = (pl.ds(0, HALF), pl.ds(HALF, HALF))
-    whole = pl.ds(0, TOKENS)
-
-    def rows_at(side, place):
-        return halves[side] if place == 8 else whole
 
     def project(chunk):
         columns = pl.ds(pl.multiple_of(chunk * HEAD_SIZE, HEAD_SIZE), HEAD_SIZE)
@@ -104,7 +101,7 @@
     def up1(side, place, half):
         way = 1 - 2 * side
         owner = ring(-way * place)
-        target = ring(-way * (place - GATHER[place]))
+        target = ring(-way * (place - PROJECT[place]))
         return remote(
             part.at[owner, halves[half]], r1.at[side, place - 1, halves[half]],
             send_sem.at[0], r1_sem.at[side, place - 1, half], (ctx, target),
@@ -120,7 +117,7 @@
         for side in both_sides:
             way = 1 - 2 * side
             owner = ring(-way * place)
-            for q in children(GATHER, place):
+            for q in children(PROJECT, place):
                 if q < 8 or side == half:
                     up1(side, q, half).wait_recv()
                     part[owner, halves[half]] += r1[side, q - 1, halves[half]]
@@ -157,13 +154,6 @@
     send1(1, 1)
 
     own_rows, prev_rows = pl.ds(TOKENS, TOKENS), pl.ds(0, TOKENS)
-    for half in range(2):
-        total = part[z, halves[half]]
-        for q in children(GATHER, 0):
-            for side in both_sides:
-                up1(side, q, half).wait_recv()
-                total = total + r1[side, q - 1, halves[half]]
-        kv[z, pl.ds(TOKENS + half * HALF, HALF)] = total.astype(BF16)
 
     def spread1(side, place, child, half):
         way = 1 - 2 * side
@@ -195,6 +185,12 @@
                 pass_on(ring(place if side else -place)).start()
 
     for half in range(2):
+        total = part[z, halves[half]]
+        for q in children(PROJECT, 0):
+            for side in both_sides:
+                up1(side, q, half).wait_recv()
+                total = total + r1[side, q - 1, halves[half]]
+        kv[z, pl.ds(TOKENS + half * HALF, HALF)] = total.astype(BF16)
         for side in both_sides:
             forward1(side, 0, half)
     pass_on(z).start()
@@ -255,69 +251,58 @@
         offset = ((k + 1) // 2) * (1 if k % 2 else -1)
         return lax.rem(z // 2 + turn * offset + KV_HEADS, KV_HEADS)
 
-    def up2(side, place):
+    def up2(side, place, half):
         way = 1 - 2 * side
-        rows = rows_at(side, place)
         target = ring(-way * (place - GATHER[place]))
         return remote(
-            s2.at[side, place - 1, rows], r2.at[side, place - 1, rows],
-            send_sem.at[5], r2_sem.at[side, place - 1], (ctx, target),
-        )
-
-    def gathered(chunk):
-        return own[chunk] + pg_dst[chunk].astype(F32)
+            s2.at[side, place - 1, halves[half]], r2.at[side, place - 1, halves[half]],
+            send_sem.at[5], r2_sem.at[side, place - 1, half], (ctx, target),
+        )
+
+    def gathered(chunk, half):
+        return own[chunk, halves[half]] + pg_dst[chunk, halves[half]].astype(F32)
+
+    def summed(side, place, half, total):
+        for q in children(GATHER, place):
+            if q < 8 or side == half:
+                up2(side, q, half).wait_recv()
+                total = total + r2[side, q - 1, halves[half]].astype(F32)
+        return total
+
+    def send2(place):
+        for half in range(2):
+            for side in both_sides:
+                if place < 8 or side == half:
+                    way = 1 - 2 * side
+                    total = summed(side, place, half, gathered(ring(8 - way * place), half))
+                    s2[side, place - 1, halves[half]] = total.astype(BF16)
+                    up2(side, place, half).start()
 
     def leaf2(k):
         send_back(head_at(k)).wait_recv()
-        place = 8 - k
-        if place in GATHER_INNER:
-            return
-        for side in both_sides:
-            way = 1 - 2 * side
-            s2[side, place - 1] = gathered(ring(8 - way * place)).astype(BF16)
-            up2(side, place).start()
-
-    def inner2(place):
-        for side in both_sides:
-            way = 1 - 2 * side
-            total = gathered(ring(8 - way * place))
-            for q in children(GATHER, place):
-                up2(side, q).wait_recv()
-                if q == 8:
-                    got = r2[side, 7, halves[side]].astype(F32)
-                    mixed = total[side * HALF : (side + 1) * HALF] + got
-                    rest = total[(1 - side) * HALF : (2 - side) * HALF]
-                    total = jnp.concatenate([rest, mixed] if side else [mixed, rest], 0)
-                else:
-                    total = total + r2[side, q - 1].astype(F32)
-            s2[side, place - 1] = total.astype(BF16)
-            up2(side, place).start()
-
-    take1(3, 1)
-    attend(head_at(0))
-    take1(6, 4, 2)
-    leaf2(0)
-    for k in (1, 2, 3):
+        if 8 - k not in GATHER_INNER:
+            send2(8 - k)
+
+    take1(3, 2, 1)
+    for k in (0, 1, 2):
         attend(head_at(k))
-    take1(7, 5, 8)
-    for k in (1, 2, 3):
+    take1(6, 5, 4)
+    for k in (0, 1, 2):
         leaf2(k)
-    for k in (4, 5, 6):
+    for k in (3, 4, 5):
         attend(head_at(k))
-    inner2(6)
-    attend(head_at(7))
+    take1(8, 7)
+    send2(6)
+    for k in (3, 4):
+        leaf2(k)
+    for k in (6, 7):
+        attend(head_at(k))
     out_q = pltpu.make_async_copy(qg_ref, qg_hbm, out_sem.at[0])
     out_q.start()
-    for k in (4, 5, 6, 7):
+    for k in (5, 6, 7):
         leaf2(k)
-    inner2(3)
-    total = gathered(ring(8))
-    for q in children(GATHER, 0):
-        for side in both_sides:
-            up2(side, q).wait_recv()
-            total = total + r2[side, q - 1].astype(F32)
+    send2(3)
     image_rows = pl.ds(pl.multiple_of(core * TOKENS, TOKENS), TOKENS)
-    kvg[z, image_rows] = total.astype(BF16)
 
     def spread2(side, place, child, half):
         way = 1 - 2 * side
@@ -352,12 +337,15 @@
                 share(ring(place if side else -place)).start()
 
     def owners_of(place):
-        return (z, ring(8)) if place == 8 else (ring(-place), ring(place))
+        if place == 0:
+            return (z,)
+        return (ring(8),) if place == 8 else (ring(-place), ring(place))
 
     def copies_c2(k):
+        lanes = pl.ds(0, HEAD_SIZE if k in (0, 8) else 2 * HEAD_SIZE)
         return [
             remote(
-                c2_src.at[k, chip_at(n)], c2_dst.at[k, n - 1],
+                c2_src.at[k, chip_at(n), :, lanes], c2_dst.at[k, n - 1, :, lanes],
                 send_sem.at[8], c2_sem.at[k, n - 1], (chip_at(n) * 2 + core, z),
             )
             for n in range(1, CHIPS)
@@ -365,24 +353,26 @@
 
     def multiply(*places):
         for place in places:
-            k = place - 1
+            k = place
             owners = owners_of(place)
             for owner in owners:
                 shared(owner)
             product = matmul(
-                ft_ref[...], jnp.concatenate([kvg[n] for n in owners], 1), ((1,), (0,))
+                ft_ref[...], jnp.concatenate([kvg[n] for n in owners], 1) if len(owners) > 1 else kvg[owners[0]], ((1,), (0,))
             )
-            c2_own[k] = product
-            c2_src[k] = product.astype(BF16).reshape(CHIPS, ROWS, 2 * HEAD_SIZE)
+            lanes = pl.ds(0, HEAD_SIZE * len(owners))
+            c2_own[k, :, lanes] = product
+            c2_src[k, :, :, lanes] = product.astype(BF16).reshape(CHIPS, ROWS, -1)
             for copy in copies_c2(k):
                 copy.start()
 
     def finish(place):
-        k = place - 1
-        total = c2_own[k, pl.ds(pl.multiple_of(chip * ROWS, ROWS), ROWS)]
+        k = place
+        lanes = pl.ds(0, HEAD_SIZE * len(owners_of(k)))
+        total = c2_own[k, pl.ds(pl.multiple_of(chip * ROWS, ROWS), ROWS), lanes]
         for n, copy in enumerate(copies_c2(k)):
             copy.wait_recv()
-            total = total + c2_dst[k, n].astype(F32)
+            total = total + c2_dst[k, n, :, lanes].astype(F32)
         total = (total * (1.0 / math.sqrt(CTX * TOKENS))).astype(BF16)
         for n, owner in enumerate(owners_of(place)):
             chunk = lax.rem(owner + 8, RING)
@@ -390,19 +380,24 @@
             wg_ref[:, columns] = total[:, n * HEAD_SIZE : (n + 1) * HEAD_SIZE]
 
     for half in range(2):
+        total = gathered(ring(8), half)
+        for side in both_sides:
+            total = summed(side, 0, half, total)
+        start = pl.multiple_of(core * TOKENS + half * HALF, HALF)
+        kvg[z, pl.ds(start, HALF)] = total.astype(BF16)
         for side in both_sides:
             forward2(side, 0, half)
     share(z).start()
     features.wait_recv()
-    take2(3, 1)
-    multiply(1, 3)
-    take2(6, 4, 2)
-    multiply(2, 4, 6)
-    take2(7, 5)
-    multiply(5, 7)
+    take2(3, 2, 1)
+    multiply(0, 3, 2, 1)
+    take2(6, 5, 4)
+    multiply(6, 5, 4)
     take2(8)
     multiply(8)
-    for place in (1, 3, 2, 4, 6, 5, 7, 8):
+    take2(7)
+    multiply(7)
+    for place in (0, 1, 3, 2, 4, 6, 5, 7, 8):
         finish(place)
     out_w = pltpu.make_async_copy(wg_ref, wg_hbm, out_sem.at[1])
     out_w.start()
@@ -417,7 +412,7 @@
         pg_src.at[fifteen],
         pg_src.at[fifteen],
         pg_src,
-        c2_dst,
+        c2_dst.at[pl.ds(0, 8)],
     )
     for n, block in enumerate(sent):
         remote(block, block, send_sem.at[n], in_sem.at[0], partner).wait_send()
@@ -463,9 +458,9 @@
             vmem((2, 8, *chunk), BF16),
             vmem((2, 8, *chunk), BF16),
             vmem((RING, *double), BF16),
-            vmem((8, 256, 2 * HEAD_SIZE), F32),
-            vmem((8, CHIPS, ROWS, 2 * HEAD_SIZE), BF16),
-            vmem((8, CHIPS - 1, ROWS, 2 * HEAD_SIZE), BF16),
+            vmem((9, 256, 2 * HEAD_SIZE), F32),
+            vmem((9, CHIPS, ROWS, 2 * HEAD_SIZE), BF16),
+            vmem((9, CHIPS - 1, ROWS, 2 * HEAD_SIZE), BF16),
             dma((5,)),
             dma((2,)),
             dma((9,)),
@@ -474,10 +469,10 @@
             dma((2, 8, 2)),
             dma((RING,)),
             dma((KV_HEADS,)),
-            dma((2, 8)),
+            dma((2, 8, 2)),
             dma((2, 8, 2)),
             dma((RING,)),
-            dma((8, CHIPS - 1)),
+            dma((9, CHIPS - 1)),
         ],
         compiler_params=pltpu.CompilerParams(
             collective_id=0, has_side_effects=True, vmem_limit_bytes=60 * 1024 * 1024

time: 94.6 us -> 90.8 us (0.960)
  Pallas kernels: 93.8 us -> 90 us
    pallas_call x1, Pallas kernels: 92.1 us -> 88.3 us  [per_device(): pl.pallas_call(kernel, out_shape=(jax.ShapeDtypeStruct(queries.shape, BF1...]
where the time goes in v3:
time: 90.8 us; the launch traced here: 90.6 us
  Pallas kernels  90 us (99%)
    pallas_call x1, Pallas kernels, per_device(): pl.pallas_call(kernel, out_shape=(jax.ShapeDtypeStruct(queries.shape, BF1...  88.3 us

profile of v3, /device:TPU:1, one launch (start us, length us, event | category | flops | bytes accessed | tf_op | source)
XLA Modules:
  0.0 90.6 jit_solution(11954606609451147616)
XLA Ops:
  0.6 88.3 %shard_map.68 = (bf16[16,8192]{1,0:T(8,128)(2,1)}, bf16[16,2048]{1,0:T(8,128)(2,1)}) custom-call(bf16[16,8192]{1,0:T(8,128)(2,1)} %q_hbm.1, bf16[128,512]{1,0:T(8,128)(2,1)} %f_hbm.1, bf16[512,2048]{1,0:T(8,128)(2,1)} %w_hbm.1, bf16[16,8192]{1,0:T(8,128)(2,1)} %g_hbm.1, s32[2,32]{1,0:T(2,128)} %bitcast.1), custom_call_target="tpu_custom_call" | custom-call | tf_op jit(solution)/shard_map/pallas_call | solution.py:434
  88.9 1.7 %shard_map.69 = (bf16[16,8192]{1,0:T(8,128)(2,1)}, bf16[16,2048]{1,0:T(8,128)(2,1)}) custom-call(bf16[16,8192]{1,0:T(8,128)(2,1)} %get-tuple-element.4.a_in, bf16[16,2048]{1,0:T(8,128)(2,1)} %get-tuple-element.5.b_in), custom_call_target="tpu_custom_call" | custom-call | tf_op jit(solution)/shard_map/pallas_call | solution.py:482

commit v4 on v3

--- a/solution.py
+++ b/solution.py
@@ -27,6 +27,10 @@
 GATHER = {3: 0, 2: 0, 1: 0, 6: 3, 5: 3, 4: 3, 8: 6, 7: 6}
 PROJECT = {3: 0, 1: 0, 6: 3, 4: 3, 2: 3, 8: 6, 7: 6, 5: 6}
 GATHER_INNER = (6, 3)
+
+OTHERS = sorted(
+    range(1, CHIPS), key=lambda n: -min(n // SIDE, SIDE - n // SIDE) - min(n % SIDE, SIDE - n % SIDE)
+)
 
 
 def children(tree, place):
@@ -283,7 +287,7 @@
         if 8 - k not in GATHER_INNER:
             send2(8 - k)
 
-    take1(3, 2, 1)
+    take1(1, 3, 2)
     for k in (0, 1, 2):
         attend(head_at(k))
     take1(6, 5, 4)
@@ -291,7 +295,7 @@
         leaf2(k)
     for k in (3, 4, 5):
         attend(head_at(k))
-    take1(8, 7)
+    take1(7, 8)
     send2(6)
     for k in (3, 4):
         leaf2(k)
@@ -348,7 +352,7 @@
                 c2_src.at[k, chip_at(n), :, lanes], c2_dst.at[k, n - 1, :, lanes],
                 send_sem.at[8], c2_sem.at[k, n - 1], (chip_at(n) * 2 + core, z),
             )
-            for n in range(1, CHIPS)
+            for n in OTHERS
         ]
 
     def multiply(*places):
@@ -370,9 +374,9 @@
         k = place
         lanes = pl.ds(0, HEAD_SIZE * len(owners_of(k)))
         total = c2_own[k, pl.ds(pl.multiple_of(chip * ROWS, ROWS), ROWS), lanes]
-        for n, copy in enumerate(copies_c2(k)):
+        for n, copy in zip(OTHERS, copies_c2(k)):
             copy.wait_recv()
-            total = total + c2_dst[k, n, :, lanes].astype(F32)
+            total = total + c2_dst[k, n - 1, :, lanes].astype(F32)
         total = (total * (1.0 / math.sqrt(CTX * TOKENS))).astype(BF16)
         for n, owner in enumerate(owners_of(place)):
             chunk = lax.rem(owner + 8, RING)

time: 90.8 us -> 90.4 us (level)
  no operation moved by 1% of the time
where the time goes in v4:
time: 90.4 us; the launch traced here: 89.8 us
  Pallas kernels  89.2 us (99%)
    pallas_call x1, Pallas kernels, per_device(): pl.pallas_call(kernel, out_shape=(jax.ShapeDtypeStruct(queries.shape, BF1...  87.5 us

profile of v4, /device:TPU:1, one launch (start us, length us, event | category | flops | bytes accessed | tf_op | source)
XLA Modules:
  0.0 89.8 jit_solution(3629031083381530741)
XLA Ops:
  0.6 87.5 %shard_map.68 = (bf16[16,8192]{1,0:T(8,128)(2,1)}, bf16[16,2048]{1,0:T(8,128)(2,1)}) custom-call(bf16[16,8192]{1,0:T(8,128)(2,1)} %q_hbm.1, bf16[128,512]{1,0:T(8,128)(2,1)} %f_hbm.1, bf16[512,2048]{1,0:T(8,128)(2,1)} %w_hbm.1, bf16[16,8192]{1,0:T(8,128)(2,1)} %g_hbm.1, s32[2,32]{1,0:T(2,128)} %bitcast.1), custom_call_target="tpu_custom_call" | custom-call | tf_op jit(solution)/shard_map/pallas_call | solution.py:438
  88.1 1.7 %shard_map.69 = (bf16[16,8192]{1,0:T(8,128)(2,1)}, bf16[16,2048]{1,0:T(8,128)(2,1)}) custom-call(bf16[16,8192]{1,0:T(8,128)(2,1)} %get-tuple-element.4.a_in, bf16[16,2048]{1,0:T(8,128)(2,1)} %get-tuple-element.5.b_in), custom_call_target="tpu_custom_call" | custom-call | tf_op jit(solution)/shard_map/pallas_call | solution.py:486
